TPU v7x, 512 devices: a whole 4x4x16 slice. The times are simulated.
512 devices in a mesh: section: 32 (over z, core), row: 16 (over y, x).
Axes of the slice: x: 4, y: 4, z: 16, core: 2. Of those that a mesh axis runs over, the one named last changes fastest.
Arguments:
- section_inputs: bfloat16 [32, 2048, 2048], P('section', 'row'), may hold values from -6 to 6
- fresh_group: bfloat16 [2048, 2048], P('row'), may hold values from -6 to 6
- resident_state: float32 [32, 8, 128, 128], P('section'), may hold values from -162.9174 to 162.9174
- qkv_weight: bfloat16 [32, 2048, 3072], P('section', 'row'), may hold values from -0.125 to 0.125
- out_weight: bfloat16 [32, 1024, 2048], P('section', 'row'), may hold values from -0.1875 to 0.1875
- input_gain: float32 [32, 2048], P('section'), may hold values from 0.1 to 1.9
- head_gain: float32 [32, 1024], P('section'), may hold values from 0.1 to 1.9
Outputs:
- section_outputs: bfloat16 [32, 2048, 2048], P('section', 'row')
- final_state: float32 [32, 8, 128, 128], P('section')
All inputs are finite; a program needn't handle non-finite values.
Results may differ from a plain program's by a relative error of at most 0.01.
Values may be sent and summed in bfloat16 or wider, within the bound.
A program may use at most 64 MiB of HBM per device.

v0:
```python
import jax
import jax.numpy as jnp
from jax import lax
from jax.sharding import PartitionSpec as P


def passed_along(value, axis, by):
    peers = lax.axis_size(axis)
    pairs = [(i, i + by) for i in range(peers) if 0 <= i + by < peers]
    return lax.ppermute(value, axis, pairs)


def layer(inputs, state, qkv_full, out_full, input_gain, head_gain):
    rows = inputs.shape[0]
    heads = state.shape[0]
    head_size = state.shape[1]
    width = heads * head_size
    wide = inputs.astype(jnp.float32)
    normed = (
        wide * lax.rsqrt(jnp.mean(wide * wide, axis=-1, keepdims=True) + 1e-05) * input_gain
    ).astype(jnp.bfloat16)
    projected = jnp.dot(normed, qkv_full, preferred_element_type=jnp.float32)
    queries = jax.nn.silu(projected[:, :width]).astype(jnp.bfloat16).reshape(rows, heads, head_size)
    key_rows = (
        jax.nn.silu(projected[:, width : 2 * width])
        .astype(jnp.bfloat16)
        .reshape(rows, heads, head_size)
    )
    value_rows = projected[:, 2 * width :].astype(jnp.bfloat16).reshape(rows, heads, head_size)
    own_state = jnp.einsum("jhd,jhe->hde", key_rows, value_rows, preferred_element_type=jnp.float32)
    every = lax.all_gather(own_state[None].astype(jnp.bfloat16), "row", axis=0, tiled=True).astype(
        jnp.float32
    )
    order = lax.iota(jnp.int32, every.shape[0])
    earlier = (order < lax.axis_index("row")).astype(jnp.float32)
    before = jnp.sum(every * earlier[:, None, None, None], axis=0)
    total = jnp.sum(every, axis=0)
    prefix = state + before
    carried = jnp.einsum("ihd,hde->ihe", queries.astype(jnp.float32), prefix)
    scores = jnp.einsum("ihd,jhd->hij", queries, key_rows, preferred_element_type=jnp.float32)
    causal = lax.broadcasted_iota(jnp.int32, (rows, rows), 0) >= lax.broadcasted_iota(
        jnp.int32, (rows, rows), 1
    )
    weights = jnp.where(causal[None], scores, 0.0).astype(jnp.bfloat16)
    local = jnp.einsum("hij,jhe->ihe", weights, value_rows, preferred_element_type=jnp.float32)
    attended = carried + local
    scaled = attended * lax.rsqrt(jnp.mean(attended * attended, axis=-1, keepdims=True) + 1e-06)
    head_out = (scaled.reshape(rows, width) * head_gain).astype(jnp.bfloat16)
    result = (wide + jnp.dot(head_out, out_full, preferred_element_type=jnp.float32)).astype(
        jnp.bfloat16
    )
    return (result, state + total)


def body(
    section_inputs, fresh_group, resident_state, qkv_weight, out_weight, input_gain, head_gain
):
    qkv_full, out_full = (
        lax.all_gather(qkv_weight[0], "row", axis=0, tiled=True),
        lax.all_gather(out_weight[0], "row", axis=0, tiled=True),
    )
    first_out, first_state = layer(
        section_inputs[0], resident_state[0], qkv_full, out_full, input_gain[0], head_gain[0]
    )
    arrived = passed_along(first_out, "section", 1)
    second_in = jnp.where(lax.axis_index("section") == 0, fresh_group, arrived)
    second_out, second_state = layer(
        second_in, first_state, qkv_full, out_full, input_gain[0], head_gain[0]
    )
    return (second_out[None], second_state[None])


def solution(mesh):
    in_specs = (
        P("section", "row", None),
        P("row", None),
        P("section", None, None, None),
        P("section", "row", None),
        P("section", "row", None),
        P("section", None),
        P("section", None),
    )
    out_specs = (P("section", "row", None), P("section", None, None, None))
    return jax.shard_map(body, mesh=mesh, in_specs=in_specs, out_specs=out_specs, check_vma=False)
```

profile of v0, /device:TPU:1, one launch (start us, length us, event | category | flops | bytes accessed | tf_op | source)
XLA Modules:
  0.0 372.2 jit_solution(13485516950461262047)
XLA Ops:
  7.2 0.7 all-gather.9.cloned.1.call-update
  7.9 1.2 fusion.32
  9.2 112.5 %all-gather.9.cloned.1.call-done = bf16[1,2048,3072]{2,1,0:T(8,128)(2,1)} async-done(((bf16[1,128,3072]{2,1,0:T(8,128)(2,1)}), bf16[1,2048,3072]{2,1,0:T(8,128)(2,1)}) %all-gather.9.cloned.1.call-update) | async-done | bytes 12582928 | tf_op jit(solution)/shard_map/all_gather | solution.py:59
  121.7 6.7 %fusion.2 = f32[128,3072]{1,0:T(8,128)S(1)} fusion(bf16[1,2048,3072]{2,1,0:T(8,128)(2,1)} %all-gather.9.cloned.1.call-done, bf16[1,128,2048]{2,1,0:T(8,128)(2,1)} %param.7, f32[2048]{0:T(1024)} %bitcast.105, f32[128]{0:T(128)S(1)} %add_rsqrt_fusion.3), kind=kOutput, calls=%fused_computation.2 | convolution fusion | flops 1611661312 | bytes 14688768 | tf_op jit(solution)/shard_map/dot_general | solution.py:22
  128.4 0.3 fusion.56
  128.7 0.2 copy.31
  128.9 0.2 copy.33
  129.1 1.0 convolution_convert_fusion.1
  130.1 0.0 all-gather.13.cloned.1.call-start
  130.1 0.7 all-gather.13.cloned.1.call-update
  130.9 66.0 %all-gather.11.cloned.1.call-done = bf16[128,128,128]{2,1,0:T(8,128)(2,1)} async-done(((bf16[8,128,128]{2,1,0:T(8,128)(2,1)}), bf16[128,128,128]{2,1,0:T(8,128)(2,1)}) %all-gather.11.cloned.1.call-update) | async-done | bytes 4194320 | tf_op jit(solution)/shard_map/all_gather | solution.py:31
  196.9 3.6 convert_reduce_fusion.1
  200.4 0.3 fusion.40
  200.8 0.5 multiply_reduce_fusion.1
  201.3 0.2 fusion.38
  201.6 65.0 %all-gather.13.cloned.1.call-done = bf16[1,1024,2048]{2,1,0:T(8,128)(2,1)} async-done(((bf16[1,64,2048]{2,1,0:T(8,128)(2,1)}), bf16[1,1024,2048]{2,1,0:T(8,128)(2,1)}) %all-gather.13.cloned.1.call-update) | async-done | bytes 4194320 | tf_op jit(solution)/shard_map/all_gather | solution.py:60
  266.5 2.9 fusion.19
  269.5 3.7 %collective-permute-start = (bf16[128,2048]{1,0:T(8,128)(2,1)S(1)}, bf16[128,2048]{1,0:T(8,128)(2,1)S(1)}, u32[]{:S(2)}, u32[]{:S(2)}) collective-permute-start(bf16[128,2048]{1,0:T(8,128)(2,1)S(1)} %fusion.19), channel_id=1, source_target_pairs={{0,16},{16,32},{32,48},{48,64},{64,80},{80,96},{96,112},{112,128},... | collective-permute-start | bytes 1572872 | tf_op jit(solution)/shard_map/ppermute | solution.py:10
  273.2 6.1 %collective-permute-done = bf16[128,2048]{1,0:T(8,128)(2,1)S(1)} collective-permute-done((bf16[128,2048]{1,0:T(8,128)(2,1)S(1)}, bf16[128,2048]{1,0:T(8,128)(2,1)S(1)}, u32[]{:S(2)}, u32[]{:S(2)}) %collective-permute-start) | collective-permute-done | bytes 524320 | tf_op jit(solution)/shard_map/ppermute | solution.py:10
  279.3 0.3 fusion.29
  279.6 6.5 %fusion = f32[128,3072]{1,0:T(8,128)S(1)} fusion(bf16[1,2048,3072]{2,1,0:T(8,128)(2,1)} %all-gather.9.cloned.1.call-done, bf16[128,2048]{1,0:T(8,128)(2,1)S(1)} %get-tuple-element.7, f32[128]{0:T(128)S(1)} %add_rsqrt_fusion.2, f32[2048]{0:T(1024)S(1)} %bitcast.106), kind=kOutput, calls=%fused_computation | convolution fusion | flops 1611661312 | bytes 14688768 | tf_op jit(solution)/shard_map/dot_general | solution.py:22
  286.1 0.3 fusion.57
  286.5 0.2 copy.32
  286.6 0.2 copy.34
  286.8 1.0 convolution_convert_fusion
  287.9 68.6 %all-gather.15.cloned.1.call-done = bf16[128,128,128]{2,1,0:T(8,128)(2,1)} async-done(((bf16[8,128,128]{2,1,0:T(8,128)(2,1)}), bf16[128,128,128]{2,1,0:T(8,128)(2,1)}) %all-gather.15.cloned.1.call-update) | async-done | bytes 4194320 | tf_op jit(solution)/shard_map/all_gather | solution.py:31
  356.5 3.5 convert_reduce_fusion
  360.0 0.9 bitcast_add_fusion
  360.9 0.3 fusion.42
  361.2 0.5 multiply_reduce_fusion
  361.8 0.2 fusion.37
  362.0 3.7 %fusion.22 = bf16[1,128,2048]{2,1,0:T(8,128)(2,1)} fusion(bf16[128,1024]{0,1:T(8,128)(2,1)S(1)} %fusion.37, bf16[1,1024,2048]{2,1,0:T(8,128)(2,1)} %all-gather.13.cloned.1.call-done, bf16[128,2048]{1,0:T(8,128)(2,1)S(1)} %get-tuple-element.7), kind=kOutput, calls=%fused_computation.18 | convolution fusion | flops 537657344 | bytes 5505024 | tf_op jit(solution)/shard_map/dot_general | solution.py:49
  (25 shorter events, 0.4 us)
Async XLA Ops:
  7.2 114.5 %all-gather.9.cloned.1.call-start = ((), (), s32[]{:S(2)}) async-start(), calls=%async_computation | async-start | bytes 13369344 | tf_op jit(solution)/shard_map/all_gather | solution.py:59
  7.9 189.0 %all-gather.11.cloned.1.call-start = ((), (), s32[]{:S(2)}) async-start(), calls=%async_computation.1 | async-start | bytes 4456448 | tf_op jit(solution)/shard_map/all_gather | solution.py:31
  128.6 71.8 %copy-start.1 = (f32[1,8,128,128]{3,2,1,0:T(8,128)S(1)}, f32[1,8,128,128]{3,2,1,0:T(8,128)}, u32[]{:S(2)}) copy-start(f32[1,8,128,128]{3,2,1,0:T(8,128)} %param.9) | copy-start | bytes 1572868
  130.1 136.5 %all-gather.13.cloned.1.call-start = ((), (), s32[]{:S(2)}) async-start(), calls=%async_computation.2 | async-start | bytes 4456448 | tf_op jit(solution)/shard_map/all_gather | solution.py:60
  130.8 225.7 %all-gather.15.cloned.1.call-start = ((), (), s32[]{:S(2)}) async-start(), calls=%async_computation.3 | async-start | bytes 4456448 | tf_op jit(solution)/shard_map/all_gather | solution.py:31
  196.9 4.5 %copy-start.4 = (f32[1,1024]{1,0:T(1,128)S(1)}, f32[1,1024]{1,0:T(1,128)}, u32[]{:S(2)}) copy-start(f32[1,1024]{1,0:T(1,128)} %param.13) | copy-start | bytes 12292
  196.9 69.7 %copy-start = (bf16[1,128,2048]{2,1,0:T(8,128)(2,1)S(1)}, bf16[1,128,2048]{2,1,0:T(8,128)(2,1)}, u32[]{:S(2)}) copy-start(bf16[1,128,2048]{2,1,0:T(8,128)(2,1)} %param.7) | copy-start | bytes 1572868
  201.2 78.1 %copy-start.2 = (bf16[128,2048]{1,0:T(8,128)(2,1)S(1)}, bf16[128,2048]{1,0:T(8,128)(2,1)}, u32[]{:S(2)}) copy-start(bf16[128,2048]{1,0:T(8,128)(2,1)} %param.8) | copy-start | bytes 1572868
  201.3 78.3 %copy-start.3 = (f32[1,2048]{1,0:T(1,128)S(1)}, f32[1,2048]{1,0:T(1,128)}, u32[]{:S(2)}) copy-start(f32[1,2048]{1,0:T(1,128)} %param.12) | copy-start | bytes 24580
  269.5 9.8 %collective-permute-start = (bf16[128,2048]{1,0:T(8,128)(2,1)S(1)}, bf16[128,2048]{1,0:T(8,128)(2,1)S(1)}, u32[]{:S(2)}, u32[]{:S(2)}) collective-permute-start(bf16[128,2048]{1,0:T(8,128)(2,1)S(1)} %fusion.19), channel_id=1, source_target_pairs={{0,16},{16,32},{32,48},{48,64},{64,80},{80,96},{96,112},{112,128},... | collective-permute-start | bytes 1572872 | tf_op jit(solution)/shard_map/ppermute | solution.py:10
Sparse Core Ops, SparseCore 0:
  11.0 110.6 all-gather.8
  130.2 66.6 all-gather.10
  199.9 66.6 all-gather.12
  288.0 68.4 all-gather.14
where the time goes:
time: 373 us; the launch traced here: 372 us
  waiting for transfers between devices  320 us (86%)
  matrix products  23.4 us (6%)
  between operations  14 us (4%)
  other arithmetic  10.6 us (3%)
  starting transfers between devices  3.89 us (1%)
    all_gather x2, waiting for transfers between devices, layer(): lax.all_gather(own_state[None].astype(jnp.bfloat16), 'row', axis=0, tiled...  135 us
    all_gather x1, waiting for transfers between devices, body(): lax.all_gather(qkv_weight[0], 'row', axis=0, tiled=True)  112 us
    all_gather x1, waiting for transfers between devices, body(): lax.all_gather(out_weight[0], 'row', axis=0, tiled=True)  65 us
    dot_general x2, matrix products, layer(): projected = jnp.dot(normed, qkv_full, preferred_element_type=jnp.float32)  13.2 us
  transfers between devices with their start and end apart: 5, of which 5 were waited for; matrix products, arithmetic and copies ran while one was open for 2% of the time, Pallas kernels for 0%

commit v1 on v0

v1 whole, which is shorter than its diff:
```python
import functools

import jax
import jax.numpy as jnp
from jax import lax
from jax.experimental import pallas as pl
from jax.experimental.pallas import tpu as pltpu
from jax.sharding import PartitionSpec as P

MESH = pl.DeviceIdType.MESH
F32 = jnp.float32
BF16 = jnp.bfloat16
SIDES = (1, 3)
IDS = {}


def slot(*key):
    return IDS.setdefault(key, len(IDS))


for _d in (1, 3, 2):
    for _p in range(3):
        slot("A", _d, _p)
for _e in range(4):
    slot("B", _e, 1), slot("B", _e, 3), slot("F", _e)
for _d in SIDES:
    for _h in range(2):
        slot("C", _d, _h), slot("D", _d, _h)
        for _c in range(4):
            slot("E", _c, _d, _h)
    slot("CF", _d), slot("DF", _d)
    for _c in range(4):
        slot("EF", _c, _d)
for _b in range(4):
    for _d in SIDES:
        slot("H", _b, _d), slot("G", _b, _d)
    slot("HF", _b), slot("GF", _b), slot("Z", _b)
for _d in (1, 2, 3):
    slot("T", 0, _d), slot("T", 1, _d), slot("R", _d), slot("H2", _d), slot("S", _d)


def kernel(
    last, x_in, fresh, state_in, w_in, wo_in, gain, hgain, out, fstate,
    wb, wof, x1, x2, nb, pj, qb, kb, vb, al, pre, run, tsum, ho, ho2s, ho2, yb, st, fs,
    ss, rs, ls,
):
    s = lax.axis_index("section")
    r = lax.axis_index("row")
    y = r // 4
    x = lax.rem(r, 4)

    def xr(d):
        return lax.rem(x + d, 4)

    def yr(d):
        return lax.rem(y + d, 4)

    def dx(d):
        return (s, y * 4 + xr(d))

    def dy(d):
        return (s, yr(d) * 4 + x)

    def rows(b):
        return pl.ds(pl.multiple_of(b * 128, 128), 128)

    def cols(j, n):
        return pl.ds(pl.multiple_of(j * n, n), n)

    makers = {}

    def define(key, src, dst, dev):
        i = IDS[key]
        makers[key] = lambda: pltpu.make_async_remote_copy(
            src_ref=src, dst_ref=dst, send_sem=ss.at[i], recv_sem=rs.at[i],
            device_id=dev, device_id_type=MESH,
        )

    def start(*key):
        makers[key]().start()

    def got(*key):
        makers[key]().wait_recv()

    def sent(*key):
        makers[key]().wait_send()

    for d in (1, 3, 2):
        for p in range(3):
            define(("A", d, p), w_in.at[:, pl.ds(pl.multiple_of(p * 1024 + xr(d) * 256, 256), 256)],
                   wb.at[r, :, pl.ds(p * 256, 256)], dx(d))
    for e in range(4):
        k = y * 4 + xr(4 - e)
        for d in SIDES:
            define(("B", e, d), wb.at[k], wb.at[k], dy(d))
        fd = 1 if e in (0, 3) else 3
        k2 = yr(4 - fd) * 4 + xr(4 - e)
        define(("F", e), wb.at[k2], wb.at[k2], dy(fd))
    for d in SIDES:
        for h in range(2):
            v = x1.at[x, pl.ds(h * 64, 64)]
            define(("C", d, h), v, v, dx(d))
            v = wof.at[r, pl.ds(h * 32, 32)]
            define(("D", d, h), v, v, dx(d))
        h = 0 if d == 1 else 1
        v = x1.at[xr(4 - d), pl.ds(h * 64, 64)]
        define(("CF", d), v, v, dx(d))
        v = wof.at[y * 4 + xr(4 - d), pl.ds(h * 32, 32)]
        define(("DF", d), v, v, dx(d))
    for c in range(4):
        for d in SIDES:
            for h in range(2):
                v = wof.at[pl.ds(y * 4 + 2 * h, 2), :, cols(xr(c), 512)]
                define(("E", c, d, h), v, v, dy(d))
            h = 0 if d == 1 else 1
            v = wof.at[pl.ds(yr(4 - d) * 4 + 2 * h, 2), :, cols(xr(c), 512)]
            define(("EF", c, d), v, v, dy(d))
    for d in (1, 2, 3):
        for t in range(2):
            define(("T", t, d), tsum.at[t, y], tsum.at[t, y], dy(d))
        define(("R", d), fresh.at[:, cols(xr(d), 512)], x2.at[xr(d), rows(x)], dx(d))
        define(("H2", d), ho2s.at[rows(xr(d))], ho2.at[x], dx(d))
        define(("S", d), fs.at[pl.ds(2 * x, 2)], fs.at[pl.ds(2 * x, 2)], dx(d))
    for b in range(4):
        rb = pl.ds(b * 128, 128)
        for d in SIDES:
            v = ho.at[x, rb]
            define(("H", b, d), v, v, dx(d))
            v = x2.at[x, rb]
            define(("G", b, d), v, v, dx(d))
        fd = 1 if b % 2 == 0 else 3
        v = ho.at[xr(4 - fd), rb]
        define(("HF", b), v, v, dx(fd))
        v = x2.at[xr(4 - fd), rb]
        define(("GF", b), v, v, dx(fd))
        define(("Z", b), yb.at[rb], x2.at[x, rb], (s + 1, r))

    loads = [
        pltpu.make_async_copy(w_in.at[:, pl.ds(pl.multiple_of(p * 1024 + x * 256, 256), 256)],
                              wb.at[r, :, pl.ds(p * 256, 256)], ls.at[p])
        for p in range(3)
    ]
    loads.append(pltpu.make_async_copy(x_in, x1.at[x], ls.at[3]))
    loads.append(pltpu.make_async_copy(wo_in, wof.at[r], ls.at[4]))
    loads.append(pltpu.make_async_copy(state_in.at[pl.ds(2 * x, 2)], st, ls.at[5]))
    for c in loads:
        c.start()
    own_fresh = pltpu.make_async_copy(fresh.at[:, cols(x, 512)], x2.at[x, rows(x)], ls.at[6])

    barrier = pltpu.get_barrier_semaphore()
    before, after = (lax.rem(s + last, last + 1), r), (lax.rem(s + 1, last + 1), r)
    for dev in [dx(1), dx(2), dx(3), dy(1), dy(2), dy(3), before, after]:
        pl.semaphore_signal(barrier, inc=1, device_id=dev, device_id_type=MESH)
    pl.semaphore_wait(barrier, 8)

    def norm_first(b):
        def strip(i, carry):
            at = pl.ds(pl.multiple_of(i * 16, 16), 16)
            v = x1[b, at, :].astype(F32)
            scale = lax.rsqrt(jnp.mean(v * v, axis=-1, keepdims=True) + 1e-05)
            n = (v * scale * gain[...]).astype(BF16)
            to = pl.ds(pl.multiple_of(b * 128 + i * 16, 16), 16)
            for p in range(4):
                nb[p, to, :] = n[:, p * 512:(p + 1) * 512]
            return carry
        lax.fori_loop(0, 8, strip, 0)

    def norm_second(b):
        def strip(i, carry):
            at = pl.ds(pl.multiple_of(b * 128 + i * 16, 16), 16)
            v = [x2[p, at, :].astype(F32) for p in range(4)]
            sq = sum(jnp.sum(u * u, axis=-1, keepdims=True) for u in v)
            scale = lax.rsqrt(sq * (1.0 / 2048) + 1e-05)
            for p in range(4):
                nb[p, at, :] = (v[p] * scale * gain[:, p * 512:(p + 1) * 512]).astype(BF16)
            return carry
        lax.fori_loop(0, 8, strip, 0)

    def project_slice(kg, first):
        for n in range(3):
            at = pl.ds(n * 256, 256)
            w = wb[pl.ds(4 * kg, 4), :, at].reshape(512, 256)
            v = jnp.dot(nb[kg], w, preferred_element_type=F32)
            if first:
                pj[:, at] = v
            else:
                pj[:, at] += v

    def project_block(b):
        rb = pl.ds(b * 128, 128)
        for n in range(3):
            at = pl.ds(n * 256, 256)
            v = jnp.zeros((128, 256), F32)
            for kg in range(4):
                w = wb[pl.ds(4 * kg, 4), :, at].reshape(512, 256)
                v += jnp.dot(nb[kg, rb, :], w, preferred_element_type=F32)
            pj[rb, at] = v

    def states(b):
        rb = rows(b)
        for h in range(2):
            at = pl.ds(h * 128, 128)
            q = pj[rb, pl.ds(h * 128, 128)]
            qb[rb, at] = (q / (1.0 + jnp.exp(-q))).astype(BF16)
            k = pj[rb, pl.ds(256 + h * 128, 128)]
            k = (k / (1.0 + jnp.exp(-k))).astype(BF16)
            kb[rb, at] = k
            v = pj[rb, pl.ds(512 + h * 128, 128)].astype(BF16)
            vb[rb, at] = v
            pre[b, h] = run[h]
            run[h] += lax.dot_general(k, v, (((0,), (0,)), ((), ())), preferred_element_type=F32)

    def local(b):
        rb = rows(b)
        keep = lax.broadcasted_iota(jnp.int32, (128, 128), 0) >= lax.broadcasted_iota(jnp.int32, (128, 128), 1)
        for h in range(2):
            at = pl.ds(h * 128, 128)
            sc = lax.dot_general(qb[rb, at], kb[rb, at], (((1,), (1,)), ((), ())), preferred_element_type=F32)
            w = jnp.where(keep, sc, 0.0).astype(BF16)
            al[rb, at] = jnp.dot(w, vb[rb, at], preferred_element_type=F32)

    def send_totals(t):
        tsum[t, y] = run[...].astype(BF16)
        for d in (1, 3, 2):
            start("T", t, d)

    def base_of(t):
        for d in (1, 3, 2):
            got("T", t, d)
        before = st[...]
        total = st[...]
        for i in range(4):
            u = tsum[t, i].astype(F32)
            before = before + u * (y > i).astype(F32)
            total = total + u
        run[...] = before
        st[...] = total

    def finish(b, put):
        rb = rows(b)
        for h in range(2):
            at = pl.ds(h * 128, 128)
            m = (run[h] + pre[b, h]).astype(BF16)
            a = al[rb, at] + jnp.dot(qb[rb, at], m, preferred_element_type=F32)
            a = a * lax.rsqrt(jnp.mean(a * a, axis=-1, keepdims=True) + 1e-06)
            g = hgain[:, pl.ds(pl.multiple_of(x * 256 + h * 128, 128), 128)]
            put(rb, at, (a * g).astype(BF16))

    def zero_run():
        run[...] = jnp.zeros_like(run)

    def loop(f):
        def step(b, carry):
            f(b)
            return carry
        lax.fori_loop(0, 4, step, 0)

    for d in (1, 3, 2):
        for p in range(3):
            start("A", d, p)
    for c in loads[:3]:
        c.wait()
    for d in SIDES:
        start("B", 0, d)
    loads[3].wait()
    norm_first(x)
    for e in (1, 3):
        for p in range(3):
            got("A", e, p)
        for d in SIDES:
            start("B", e, d)
    for d, h in ((1, 0), (3, 1), (1, 1), (3, 0)):
        start("C", d, h)
    for p in range(3):
        got("A", 2, p)
    for d in SIDES:
        start("B", 2, d)

    def forward_w(e):
        fd = 1 if e in (0, 3) else 3
        got("B", e, fd)
        start("F", e)

    forward_w(0)
    forward_w(1)
    got("C", 1, 0)
    start("CF", 1)
    got("C", 3, 1)
    start("CF", 3)
    loads[4].wait()
    for d, h in ((1, 0), (3, 1), (1, 1), (3, 0)):
        start("D", d, h)
    forward_w(3)
    forward_w(2)
    got("C", 1, 1)
    norm_first(xr(3))
    got("C", 3, 0)
    norm_first(xr(1))
    for e in range(4):
        got("B", e, 3 if e in (0, 3) else 1)
    got("D", 1, 0)
    start("DF", 1)
    got("D", 3, 1)
    start("DF", 3)

    @pl.when(s == 0)
    def _():
        own_fresh.start()
        for d in (1, 3, 2):
            start("R", d)

    got("CF", 1)
    got("CF", 3)
    norm_first(xr(2))
    project_slice(y, True)
    project_slice(yr(3), False)
    project_slice(yr(1), False)
    for e in range(4):
        got("F", e)
    project_slice(yr(2), False)

    zero_run()
    loop(states)
    send_totals(0)
    got("D", 1, 1)
    got("D", 3, 0)
    got("DF", 1)
    got("DF", 3)
    for d, h in ((1, 0), (3, 1), (1, 1), (3, 0)):
        start("E", 0, d, h)
    loop(local)
    loads[5].wait()
    base_of(0)

    def put_first(rb, at, v):
        ho[x, rb, at] = v

    for b in range(4):
        finish(b, put_first)
        for d in SIDES:
            start("H", b, d)
    got("E", 0, 1, 0)
    start("EF", 0, 1)
    got("E", 0, 3, 1)
    start("EF", 0, 3)
    got("E", 0, 1, 1)
    got("E", 0, 3, 0)
    for c in range(1, 4):
        for d, h in ((1, 0), (3, 1), (1, 1), (3, 0)):
            start("E", c, d, h)

    def forward_h(b):
        got("H", b, 1)
        got("H", b, 3)
        start("HF", b)

    def out_first(b):
        got("HF", b)
        rb = pl.ds(b * 128, 128)
        for n in range(2):
            at = pl.ds(pl.multiple_of(x * 512 + n * 256, 256), 256)
            v = x1[b, :, at].astype(F32)
            for j in range(4):
                w = wof[pl.ds(4 * j, 4), :, at].reshape(256, 256)
                v += jnp.dot(ho[j, rb, :], w, preferred_element_type=F32)
            yb[rb, pl.ds(n * 256, 256)] = v.astype(BF16)

        @pl.when(s < last)
        def _():
            start("Z", b)

    def gather_second(b):
        @pl.when(s > 0)
        def _():
            got("Z", b)

        for d in SIDES:
            start("G", b, d)

    def forward_g(b):
        got("G", b, 1)
        got("G", b, 3)
        start("GF", b)

    def second(b):
        got("GF", b)
        norm_second(b)
        project_block(b)
        states(b)

    @pl.when(s == 0)
    def _():
        own_fresh.wait()
        for d in (1, 3, 2):
            got("R", d)

    forward_h(0)
    forward_h(1)
    got("EF", 0, 1)
    got("EF", 0, 3)
    out_first(0)
    forward_h(2)
    out_first(1)
    gather_second(0)
    forward_h(3)
    out_first(2)
    gather_second(1)
    out_first(3)
    forward_g(0)
    gather_second(2)
    gather_second(3)
    for c in range(1, 4):
        got("E", c, 1, 0)
        start("EF", c, 1)
        got("E", c, 3, 1)
        start("EF", c, 3)
    forward_g(1)
    zero_run()
    second(0)
    forward_g(2)
    second(1)
    forward_g(3)
    second(2)
    second(3)

    send_totals(1)
    loop(local)
    base_of(1)
    fs[pl.ds(2 * x, 2)] = st[...].astype(BF16)

    def put_second(rb, at, v):
        ho2s[rb, at] = v

    for d in (2, 1, 3):
        finish(xr(d), put_second)
        start("H2", d)
    for d in (2, 1, 3):
        start("S", d)

    def put_own(rb, at, v):
        ho2[x, :, at] = v

    finish(x, put_own)
    for c in range(1, 4):
        got("E", c, 1, 1)
        got("E", c, 3, 0)
        got("EF", c, 1)
        got("EF", c, 3)
    for d in (1, 3, 2):
        got("H2", d)
    for n in range(8):
        at = pl.ds(n * 256, 256)
        v = x2[n // 2, rows(x), pl.ds((n % 2) * 256, 256)].astype(F32)
        for j in range(4):
            w = wof[pl.ds(4 * j, 4), :, at].reshape(256, 256)
            v += jnp.dot(ho2[j], w, preferred_element_type=F32)
        out[:, at] = v.astype(BF16)
    for d in (1, 3, 2):
        got("S", d)
    fstate[...] = fs[...].astype(F32)

    for key in IDS:
        if key[0] == "Z":
            @pl.when(s < last)
            def _():
                sent(*key)
        elif key[0] == "R":
            @pl.when(s == 0)
            def _():
                sent(*key)
        else:
            sent(*key)


def body(section_inputs, fresh_group, resident_state, qkv_weight, out_weight, input_gain, head_gain):
    anywhere = pl.BlockSpec(memory_space=pl.ANY)
    vmem = pl.BlockSpec(memory_space=pltpu.VMEM)
    n = len(IDS)
    out, state = pl.pallas_call(
        functools.partial(kernel, lax.axis_size("section") - 1),
        name="two_ticks",
        out_shape=(
            jax.ShapeDtypeStruct((128, 2048), BF16),
            jax.ShapeDtypeStruct((8, 128, 128), F32),
        ),
        in_specs=[anywhere] * 5 + [vmem] * 2,
        out_specs=(vmem, vmem),
        scratch_shapes=[
            pltpu.VMEM((16, 128, 768), BF16),
            pltpu.VMEM((16, 64, 2048), BF16),
            pltpu.VMEM((4, 128, 2048), BF16),
            pltpu.VMEM((4, 512, 512), BF16),
            pltpu.VMEM((4, 512, 512), BF16),
            pltpu.VMEM((512, 768), F32),
            pltpu.VMEM((512, 256), BF16),
            pltpu.VMEM((512, 256), BF16),
            pltpu.VMEM((512, 256), BF16),
            pltpu.VMEM((512, 256), F32),
            pltpu.VMEM((4, 2, 128, 128), F32),
            pltpu.VMEM((2, 128, 128), F32),
            pltpu.VMEM((2, 4, 2, 128, 128), BF16),
            pltpu.VMEM((4, 512, 256), BF16),
            pltpu.VMEM((512, 256), BF16),
            pltpu.VMEM((4, 128, 256), BF16),
            pltpu.VMEM((512, 512), BF16),
            pltpu.VMEM((2, 128, 128), F32),
            pltpu.VMEM((8, 128, 128), BF16),
            pltpu.SemaphoreType.DMA((n,)),
            pltpu.SemaphoreType.DMA((n,)),
            pltpu.SemaphoreType.DMA((7,)),
        ],
        compiler_params=pltpu.CompilerParams(
            collective_id=0, has_side_effects=True, vmem_limit_bytes=48 * 2**20
        ),
        cost_estimate=pl.CostEstimate(flops=4_600_000_000, bytes_accessed=4_000_000, transcendentals=0),
    )(
        section_inputs[0], fresh_group, resident_state[0], qkv_weight[0], out_weight[0], input_gain, head_gain
    )
    return (out[None], state[None])


def solution(mesh):
    in_specs = (
        P("section", "row", None),
        P("row", None),
        P("section", None, None, None),
        P("section", "row", None),
        P("section", "row", None),
        P("section", None),
        P("section", None),
    )
    out_specs = (P("section", "row", None), P("section", None, None, None))
    return jax.shard_map(body, mesh=mesh, in_specs=in_specs, out_specs=out_specs, check_vma=False)
```

time: 373 us -> 109 us (0.29)
  waiting for transfers between devices: 320 us -> 0 us
  Pallas kernels: 0 us -> 99.9 us
  matrix products: 23.4 us -> 0 us
  between operations: 14 us -> 0.66 us
  other arithmetic: 10.6 us -> 0 us
  local copies, waits for them, and re-layouts: 0.77 us -> 8.17 us
  starting transfers between devices: 3.89 us -> 0 us
    all_gather x4 -> x0, waiting for transfers between devices: 312 us -> none  [the longest x2 135 us: layer(): lax.all_gather(own_state[None].astype(jnp.bfloat16), 'row', axis=0, tiled...]
    pallas_call x0 -> x1, Pallas kernels: none -> 99.9 us  [body(): pl.pallas_call(functools.partial(kernel, lax.axis_size('section') - 1), n...]
    dot_general x10 -> x0, matrix products: 23.4 us -> none  [the longest x2 13.2 us: layer(): projected = jnp.dot(normed, qkv_full, preferred_element_type=jnp.float32)]
    reduce_sum x4 -> x0, other arithmetic: 8.6 us -> none  [the longest x2 7.09 us: layer(): total = jnp.sum(every, axis=0)]
    unnamed x10 -> x16, local copies, waits for them, and re-layouts: 0.03 us -> 8.17 us
    ppermute x1 -> x0, waiting for transfers between devices: 6.1 us -> none  [passed_along(): return lax.ppermute(value, axis, pairs)]
    ppermute x1 -> x0, starting transfers between devices: 3.74 us -> none  [passed_along(): return lax.ppermute(value, axis, pairs)]
  transfers between devices with their start and end apart: 5 -> 0, of which waited for: 5 -> 0; matrix products, arithmetic and copies ran while one was open for 2% -> 0% of each run, Pallas kernels for 0% -> 0%
where the time goes in v1:
time: 109 us
  Pallas kernels  99.9 us (92%)
  local copies, waits for them, and re-layouts  8.17 us (7%)
    pallas_call x1, Pallas kernels, body(): pl.pallas_call(functools.partial(kernel, lax.axis_size('section') - 1), n...  99.9 us
    unnamed x16, local copies, waits for them, and re-layouts  8.17 us

profile of v1, /device:TPU:1, one launch (start us, length us, event | category | flops | bytes accessed | tf_op | source)
XLA Modules:
  0.0 108.7 jit_solution(395876756289116739)
XLA Ops:
  0.6 0.0 copy-start.6
  0.6 0.7 copy-done.6
  1.3 0.0 copy-start
  1.3 1.1 %copy-done = bf16[1,128,3072]{2,1,0:T(8,128)(2,1)S(1)} copy-done((bf16[1,128,3072]{2,1,0:T(8,128)(2,1)S(1)}, bf16[1,128,3072]{2,1,0:T(8,128)(2,1)}, u32[]{:S(2)}) %copy-start) | copy-done | bytes 786456
  2.5 0.0 copy-start.1
  2.5 1.0 copy-done.1
  3.5 0.0 copy-start.2
  3.5 1.0 copy-done.2
  4.5 0.0 copy-start.3
  4.5 1.0 copy-done.3
  5.6 0.0 copy-start.4
  5.6 0.9 copy-done.4
  6.5 0.0 copy-start.5
  6.5 0.7 copy-done.5
  7.2 99.9 %two_ticks.1 = (bf16[128,2048]{1,0:T(8,128)(2,1)S(1)}, f32[8,128,128]{2,1,0:T(8,128)S(1)}) custom-call(bf16[128,2048]{1,0:T(8,128)(2,1)S(1)} %bitcast.9, bf16[128,2048]{1,0:T(8,128)(2,1)S(1)} %copy-done.2, f32[8,128,128]{2,1,0:T(8,128)S(1)} %bitcast.10, bf16[128,3072]{1,0:T(8,128)(2,1)S(1)} %bitcast.8, bf16[64,2048]{1,0:T(8,128)(2,1)S(1)} %bitcast.11, ...), custom_call_target="tpu_custom_call" | custom-call | flops 4600000000 | bytes 4000000 | tf_op jit(solution)/shard_map/two_ticks/pallas_call | solution.py:479
  107.1 0.8 copy.11
  107.9 0.8 copy.12
Async XLA Ops:
  0.6 0.7 copy-start.6
  1.3 1.1 %copy-start = (bf16[1,128,3072]{2,1,0:T(8,128)(2,1)S(1)}, bf16[1,128,3072]{2,1,0:T(8,128)(2,1)}, u32[]{:S(2)}) copy-start(bf16[1,128,3072]{2,1,0:T(8,128)(2,1)} %param.10) | copy-start | bytes 2359300
  2.5 1.0 copy-start.1
  3.5 1.0 copy-start.2
  4.5 1.0 copy-start.3
  5.6 0.9 copy-start.4
  6.5 0.7 copy-start.5

commit v2 on v0

v2 whole, which is shorter than its diff:
```python
import functools

import jax
import jax.numpy as jnp
from jax import lax
from jax.experimental import pallas as pl
from jax.experimental.pallas import tpu as pltpu
from jax.sharding import PartitionSpec as P

MESH = pl.DeviceIdType.MESH
F32 = jnp.float32
BF16 = jnp.bfloat16
SIDES = (1, 3)
OTHERS = (1, 3, 2)
STAGES = 2
PART = 128 // STAGES
IDS = {}


def slot(*key):
    return IDS.setdefault(key, len(IDS))


for _d in OTHERS:
    for _p in range(3):
        slot("A", _d, _p)
    slot("D", _d), slot("S", _d), slot("T", 0, _d), slot("T", 1, _d)
slot("X")
for _e in range(4):
    for _d in SIDES:
        slot("B", _e, _d), slot("E", _e, _d)
    slot("F", _e), slot("EF", _e)
for _d in SIDES:
    for _h in range(2):
        slot("C", _d, _h)
    slot("CF", _d)
for _q in range(STAGES):
    for _t in range(2):
        for _d in SIDES:
            slot("H", _t, _q, _d)
        slot("HF", _t, _q)
    for _d in SIDES:
        slot("G", _q, _d)
    slot("GF", _q)
    for _d in range(4):
        slot("Z", _q, _d), slot("O", _q, _d)


def kernel(
    last, x_in, fresh, state_in, w_in, wo_in, gain_in, hgain_in, out, fstate,
    wb, wos, x1, x2, nb, pj, qb, kb, vb, al, pre, run, tsum, ho, yb, st, gain, hgain,
    ss, rs, ls,
):
    s = lax.axis_index("section")
    r = lax.axis_index("row")
    odd = lax.rem(s, 2)
    py = r // 4
    px = lax.rem(r, 4)
    g = py + odd * (px - py)
    u = px + odd * (py - px)

    def ur(d):
        return lax.rem(u + d, 4)

    def gr(d):
        return lax.rem(g + d, 4)

    def row_of(gg, uu):
        return gg * (4 - 3 * odd) + uu * (1 + 3 * odd)

    def row_of_next(gg, uu):
        return gg * (1 + 3 * odd) + uu * (4 - 3 * odd)

    def du(d):
        return (s, row_of(g, ur(d)))

    def dg(d):
        return (s, row_of(gr(d), u))

    def cols(j, n):
        return pl.ds(pl.multiple_of(j * n, n), n)

    def part(q):
        return pl.ds(q * PART, PART)

    before = lax.rem(s + last, last + 1)
    after = lax.rem(s + 1, last + 1)
    makers = {}

    def define(key, src, dst, dev):
        i = IDS[key]
        makers[key] = lambda: pltpu.make_async_remote_copy(
            src_ref=src, dst_ref=dst, send_sem=ss.at[i], recv_sem=rs.at[i],
            device_id=dev, device_id_type=MESH,
        )

    def start(*key):
        makers[key]().start()

    def got(*key):
        makers[key]().wait_recv()

    def sent(*key):
        makers[key]().wait_send()

    for d in OTHERS:
        for p in range(3):
            define(("A", d, p), w_in.at[:, pl.ds(pl.multiple_of(p * 1024 + ur(d) * 256, 256), 256)],
                   wb.at[g, u, :, pl.ds(p * 256, 256)], du(d))
        define(("D", d), wo_in.at[:, cols(ur(d), 512)], wos.at[r], du(d))
        for t in range(2):
            define(("T", t, d), tsum.at[t, g], tsum.at[t, g], dg(d))
        v = fstate.at[pl.ds(2 * u, 2)]
        define(("S", d), v, v, du(d))
    for e in range(4):
        src = ur(4 - e)
        fd = 1 if e in (0, 3) else 3
        for d in SIDES:
            v = wb.at[g, src]
            define(("B", e, d), v, v, dg(d))
            v = wos.at[row_of(g, src)]
            define(("E", e, d), v, v, dg(d))
        v = wb.at[gr(4 - fd), src]
        define(("F", e), v, v, dg(fd))
        v = wos.at[row_of(gr(4 - fd), src)]
        define(("EF", e), v, v, dg(fd))
    for d in SIDES:
        for h in range(2):
            v = x1.at[u, pl.ds(h * 64, 64)]
            define(("C", d, h), v, v, du(d))
        v = x1.at[ur(4 - d), pl.ds((0 if d == 1 else 1) * 64, 64)]
        define(("CF", d), v, v, du(d))
    for q in range(STAGES):
        fd = SIDES[q % 2]
        for t in range(2):
            for d in SIDES:
                v = ho.at[t, u, :, part(q)]
                define(("H", t, q, d), v, v, du(d))
            v = ho.at[t, ur(4 - fd), :, part(q)]
            define(("HF", t, q), v, v, du(fd))
        for d in SIDES:
            v = x2.at[u, part(q)]
            define(("G", q, d), v, v, du(d))
        v = x2.at[ur(4 - fd), part(q)]
        define(("GF", q), v, v, du(fd))
        for d in range(4):
            define(("Z", q, d), yb.at[0, ur(d), part(q)], x2.at[ur(d), part(q), cols(u, 512)],
                   (after, row_of_next(g, ur(d))))
            define(("O", q, d), yb.at[1, ur(d), part(q)], out.at[part(q), cols(u, 512)], (s, 4 * g + ur(d)))
    apart = odd * (g - u) != 0
    here = odd * (g - u) == 0
    define(("X",), x_in, x1.at[g], (s, 4 * g + u))

    loads = [
        pltpu.make_async_copy(w_in.at[:, pl.ds(pl.multiple_of(p * 1024 + u * 256, 256), 256)],
                              wb.at[g, u, :, pl.ds(p * 256, 256)], ls.at[p])
        for p in range(3)
    ]
    own_block = pltpu.make_async_copy(x_in, x1.at[u], ls.at[3])
    loads.append(pltpu.make_async_copy(wo_in.at[:, cols(u, 512)], wos.at[r], ls.at[4]))
    loads.append(pltpu.make_async_copy(state_in.at[pl.ds(2 * u, 2)], st, ls.at[5]))
    loads.append(pltpu.make_async_copy(gain_in, gain, ls.at[6]))
    loads.append(pltpu.make_async_copy(hgain_in, hgain, ls.at[7]))
    own_fresh = pltpu.make_async_copy(fresh, x2.at[u], ls.at[8])
    for c in loads:
        c.start()

    @pl.when(here)
    def _():
        own_block.start()

    @pl.when(s == 0)
    def _():
        own_fresh.start()

    barrier = pltpu.get_barrier_semaphore()
    for dev in [(s, lax.rem(r + d, 16)) for d in range(1, 16)] + [(before, row_of_next(g, ur(d))) for d in range(4)]:
        pl.semaphore_signal(barrier, inc=1, device_id=dev, device_id_type=MESH)
    pl.semaphore_wait(barrier, 19)

    def norm(xs, b, low, count):
        def strip(i, carry):
            at = pl.ds(pl.multiple_of(low + i * 16, 16), 16)
            v = xs[b, at, :].astype(F32)
            v = v * lax.rsqrt(jnp.mean(v * v, axis=-1, keepdims=True) + 1e-05)
            for k in range(16):
                g2 = k // 4 + odd * (k % 4 - k // 4)
                u2 = k % 4 + odd * (k // 4 - k % 4)
                ks = slice(k * 128, k * 128 + 128)
                nb[g2, b, at, cols(u2, 128)] = (v[:, ks] * gain[:, ks]).astype(BF16)
            return carry
        lax.fori_loop(0, count // 16, strip, 0, unroll=4)

    def keep_projected(n, v, at):
        if n < 2:
            v = v / (1.0 + jnp.exp(-v))
        [qb, kb, vb][n][:, at, :] = v.astype(BF16).reshape(4, -1, 256)

    def project_slice(g2, first=False, final=False):
        def one(i, carry):
            at = pl.ds(pl.multiple_of(i * 64, 64), 64)
            for n in range(3):
                to = pl.ds(n * 256, 256)
                w = wb[g2, :, :, to].reshape(512, 256)
                v = jnp.dot(nb[g2, :, at].reshape(256, 512), w, preferred_element_type=F32)
                if not first:
                    v += pj[:, at, to].reshape(256, 256)
                if final:
                    keep_projected(n, v, at)
                else:
                    pj[:, at, to] = v.reshape(4, 64, 256)
            return carry
        lax.fori_loop(0, 2, one, 0)

    def project_stage(q):
        for n in range(3):
            to = pl.ds(n * 256, 256)
            v = jnp.zeros((4 * PART, 256), F32)
            for g2 in range(4):
                w = wb[g2, :, :, to].reshape(512, 256)
                v += jnp.dot(nb[g2, :, part(q)].reshape(4 * PART, 512), w, preferred_element_type=F32)
            keep_projected(n, v, part(q))

    def states(t):
        for h in range(2):
            at = pl.ds(h * 128, 128)
            total = jnp.zeros((128, 128), F32)
            for b in range(4):
                pre[b, h] = total
                total += lax.dot_general(
                    kb[b, :, at], vb[b, :, at], (((0,), (0,)), ((), ())), preferred_element_type=F32
                )
            tsum[t, g, h] = total.astype(BF16)
        for d in OTHERS:
            start("T", t, d)

    def local():
        keep = lax.broadcasted_iota(jnp.int32, (128, 128), 0) >= lax.broadcasted_iota(jnp.int32, (128, 128), 1)
        for b in range(4):
            for h in range(2):
                at = pl.ds(h * 128, 128)
                sc = lax.dot_general(qb[b, :, at], kb[b, :, at], (((1,), (1,)), ((), ())), preferred_element_type=F32)
                w = jnp.where(keep, sc, 0.0).astype(BF16)
                al[b, :, at] = jnp.dot(w, vb[b, :, at], preferred_element_type=F32)

    def prefixes(t):
        for d in OTHERS:
            got("T", t, d)
        for h in range(2):
            ahead = st[h]
            whole = ahead
            for j in range(4):
                v = tsum[t, j, h].astype(F32)
                ahead = ahead + v * (j < g).astype(F32)
                whole = whole + v
            run[h] = ahead
            st[h] = whole

    def finish(t):
        for b in range(4):
            for h in range(2):
                at = pl.ds(h * 128, 128)
                m = (run[h] + pre[b, h]).astype(BF16)
                a = al[b, :, at] + jnp.dot(qb[b, :, at], m, preferred_element_type=F32)
                a = a * lax.rsqrt(jnp.mean(a * a, axis=-1, keepdims=True) + 1e-06)
                w = hgain[:, pl.ds(pl.multiple_of(u * 256 + h * 128, 128), 128)]
                ho[t, u, b, :, at] = (a * w).astype(BF16)
        for q in range(STAGES):
            for d in SIDES:
                start("H", t, q, d)

    def forward_h(t, q):
        for d in SIDES:
            got("H", t, q, d)
        start("HF", t, q)

    def project_out(t, xs, q):
        got("HF", t, q)
        for n in range(2):
            at = pl.ds(n * 256, 256)
            v = xs[:, part(q), pl.ds(pl.multiple_of(u * 512 + n * 256, 256), 256)].astype(F32).reshape(4 * PART, 256)
            for j in range(4):
                w = wos[4 * j:4 * j + 4, :, at].reshape(256, 256)
                v += jnp.dot(ho[t, j, :, part(q)].reshape(4 * PART, 256), w, preferred_element_type=F32)
            yb[t, :, part(q), at] = v.astype(BF16).reshape(4, PART, 256)

    for d in OTHERS:
        for p in range(3):
            start("A", d, p)

    @pl.when(apart)
    def _():
        start("X")

    for c in loads[:3]:
        c.wait()
    for d in SIDES:
        start("B", 0, d)
    loads[5].wait()
    for e in (1, 3):
        for p in range(3):
            got("A", e, p)
        for d in SIDES:
            start("B", e, d)

    @pl.when(here)
    def _():
        own_block.wait()

    @pl.when(apart)
    def _():
        got("X")

    for d, h in ((1, 0), (3, 1), (1, 1), (3, 0)):
        start("C", d, h)
    norm(x1, u, 0, 128)
    for p in range(3):
        got("A", 2, p)
    for d in SIDES:
        start("B", 2, d)

    def forward_w(e):
        got("B", e, 1 if e in (0, 3) else 3)
        start("F", e)

    forward_w(0)
    forward_w(1)
    got("C", 1, 0)
    start("CF", 1)
    got("C", 3, 1)
    start("CF", 3)
    forward_w(3)
    forward_w(2)
    got("C", 1, 1)
    norm(x1, ur(3), 0, 128)
    got("C", 3, 0)
    norm(x1, ur(1), 0, 128)
    for d in OTHERS:
        start("D", d)
    for e in range(4):
        got("B", e, 3 if e in (0, 3) else 1)
    got("CF", 1)
    got("CF", 3)
    norm(x1, ur(2), 0, 128)
    project_slice(g, first=True)
    project_slice(gr(3))
    project_slice(gr(1))
    loads[3].wait()
    for e in (0, 1, 3, 2):
        if e:
            got("D", e)
        for d in SIDES:
            start("E", e, d)
    for e in range(4):
        got("F", e)
    project_slice(gr(2), final=True)

    states(0)
    local()

    def forward_e(e):
        got("E", e, 1 if e in (0, 3) else 3)
        start("EF", e)

    for e in (0, 1, 3, 2):
        forward_e(e)
    loads[4].wait()
    loads[6].wait()
    prefixes(0)
    finish(0)
    for q in range(STAGES):
        forward_h(0, q)
    for e in range(4):
        got("E", e, 3 if e in (0, 3) else 1)
        got("EF", e)
    for q in range(STAGES):
        project_out(0, x1, q)

        @pl.when(s < last)
        def _():
            for d in (2, 1, 3, 0):
                start("Z", q, d)

    for q in range(STAGES):
        if q == 0:
            @pl.when(s == 0)
            def _():
                own_fresh.wait()

        @pl.when(s > 0)
        def _():
            for d in range(4):
                got("Z", q, d)

        for d in SIDES:
            start("G", q, d)
    for q in range(STAGES):
        for d in SIDES:
            got("G", q, d)
        start("GF", q)
    for q in range(STAGES):
        for d in (0, 1, 3):
            norm(x2, ur(d), q * PART, PART)
        got("GF", q)
        norm(x2, ur(2), q * PART, PART)
        project_stage(q)
    states(1)
    local()
    prefixes(1)
    fstate[pl.ds(2 * u, 2)] = st[...].astype(BF16)
    for d in OTHERS:
        start("S", d)
    finish(1)
    for q in range(STAGES):
        forward_h(1, q)
    for q in range(STAGES):
        project_out(1, x2, q)
        for d in (2, 1, 3):
            start("O", q, d)

        @pl.when(apart)
        def _():
            start("O", q, 0)

    @pl.when(here)
    def _():
        out[:, cols(u, 512)] = yb[1, u]

    for q in range(STAGES):
        for d in (2, 1, 3):
            got("O", q, d)

    @pl.when(apart)
    def _():
        for q in range(STAGES):
            got("O", q, 0)

    for d in OTHERS:
        got("S", d)
    for key in IDS:
        if key[0] == "Z":
            @pl.when(s < last)
            def _():
                sent(*key)
        elif key[0] == "X" or (key[0] == "O" and key[2] == 0):
            @pl.when(apart)
            def _():
                sent(*key)
        else:
            sent(*key)


def body(section_inputs, fresh_group, resident_state, qkv_weight, out_weight, input_gain, head_gain):
    anywhere = pl.BlockSpec(memory_space=pl.ANY)
    vmem = pl.BlockSpec(memory_space=pltpu.VMEM)
    n = len(IDS)
    out, state = pl.pallas_call(
        functools.partial(kernel, lax.axis_size("section") - 1),
        name="two_ticks",
        out_shape=(
            jax.ShapeDtypeStruct((128, 2048), BF16),
            jax.ShapeDtypeStruct((8, 128, 128), BF16),
        ),
        in_specs=[anywhere] * 7,
        out_specs=(vmem, vmem),
        scratch_shapes=[
            pltpu.VMEM((4, 4, 128, 768), BF16),
            pltpu.VMEM((16, 64, 512), BF16),
            pltpu.VMEM((4, 128, 2048), BF16),
            pltpu.VMEM((4, 128, 2048), BF16),
            pltpu.VMEM((4, 4, 128, 512), BF16),
            pltpu.VMEM((4, 128, 768), F32),
            pltpu.VMEM((4, 128, 256), BF16),
            pltpu.VMEM((4, 128, 256), BF16),
            pltpu.VMEM((4, 128, 256), BF16),
            pltpu.VMEM((4, 128, 256), F32),
            pltpu.VMEM((4, 2, 128, 128), F32),
            pltpu.VMEM((2, 128, 128), F32),
            pltpu.VMEM((2, 4, 2, 128, 128), BF16),
            pltpu.VMEM((2, 4, 4, 128, 256), BF16),
            pltpu.VMEM((2, 4, 128, 512), BF16),
            pltpu.VMEM((2, 128, 128), F32),
            pltpu.VMEM((1, 2048), F32),
            pltpu.VMEM((1, 1024), F32),
            pltpu.SemaphoreType.DMA((n,)),
            pltpu.SemaphoreType.DMA((n,)),
            pltpu.SemaphoreType.DMA((9,)),
        ],
        compiler_params=pltpu.CompilerParams(
            collective_id=0, has_side_effects=True, vmem_limit_bytes=61 * 2**20
        ),
        cost_estimate=pl.CostEstimate(flops=4_600_000_000, bytes_accessed=4_000_000, transcendentals=0),
    )(
        section_inputs[0], fresh_group, resident_state[0], qkv_weight[0], out_weight[0], input_gain, head_gain
    )
    return (out[None], state.astype(F32)[None])


def solution(mesh):
    in_specs = (
        P("section", "row", None),
        P("row", None),
        P("section", None, None, None),
        P("section", "row", None),
        P("section", "row", None),
        P("section", None),
        P("section", None),
    )
    out_specs = (P("section", "row", None), P("section", None, None, None))
    return jax.shard_map(body, mesh=mesh, in_specs=in_specs, out_specs=out_specs, check_vma=False)
```

time: 373 us -> 129 us (0.35)
  the two profiles are of different devices: /device:TPU:1 before, /device:TPU:392 now
where the time goes in v2:
time: 129 us
  Pallas kernels  125 us (97%)
  other arithmetic  1.84 us (1%)
    pallas_call x1, Pallas kernels, body(): pl.pallas_call(functools.partial(kernel, lax.axis_size('section') - 1), n...  125 us

profile of v2, /device:TPU:392, one launch (start us, length us, event | category | flops | bytes accessed | tf_op | source)
XLA Modules:
  0.0 128.6 jit_solution(6147654376117714017)
XLA Ops:
  0.6 125.3 %two_ticks.1 = (bf16[128,2048]{1,0:T(8,128)(2,1)}, bf16[8,128,128]{2,1,0:T(8,128)(2,1)}) custom-call(bf16[128,2048]{1,0:T(8,128)(2,1)} %bitcast.10, bf16[128,2048]{1,0:T(8,128)(2,1)} %fresh.1, f32[8,128,128]{2,1,0:T(8,128)} %bitcast.11, bf16[128,3072]{1,0:T(8,128)(2,1)} %bitcast.9, bf16[64,2048]{1,0:T(8,128)(2,1)} %bitcast.12, f32[1,2048]{1,0:T(1,128)} %gain_in.1, ...), custom_call_target="tpu_custom_call" | custom-call | flops 4600000000 | bytes 4000000 | tf_op jit(solution)/shard_map/two_ticks/pallas_call | solution.py:457
  125.9 0.0 copy-start
  126.0 1.8 %bitcast_convert_fusion = f32[1,8,128,128]{3,2,1,0:T(8,128)} fusion(bf16[8,128,128]{2,1,0:T(8,128)(2,1)} %get-tuple-element.5), kind=kLoop, calls=%fused_computation | loop fusion | flops 131072 | bytes 786432 | tf_op jit(solution)/shard_map/broadcast_in_dim | solution.py:496
  127.8 0.0 copy-done
  127.8 0.8 copy.10
Async XLA Ops:
  125.9 1.8 %copy-start = (bf16[128,2048]{1,0:T(8,128)(2,1)S(1)}, bf16[128,2048]{1,0:T(8,128)(2,1)}, u32[]{:S(2)}) copy-start(bf16[128,2048]{1,0:T(8,128)(2,1)} %get-tuple-element.4) | copy-start | bytes 1572868

commit v3 on v1

--- a/solution.py
+++ b/solution.py
@@ -23,13 +23,14 @@
         slot("A", _d, _p)
 for _e in range(4):
     slot("B", _e, 1), slot("B", _e, 3), slot("F", _e)
+    slot("K", _e, 1), slot("K", _e, 3), slot("KF", _e)
 for _d in SIDES:
     for _h in range(2):
         slot("C", _d, _h), slot("D", _d, _h)
-        for _c in range(4):
+        for _c in range(1, 4):
             slot("E", _c, _d, _h)
     slot("CF", _d), slot("DF", _d)
-    for _c in range(4):
+    for _c in range(1, 4):
         slot("EF", _c, _d)
 for _b in range(4):
     for _d in SIDES:
@@ -40,8 +41,8 @@
 
 
 def kernel(
-    last, x_in, fresh, state_in, w_in, wo_in, gain, hgain, out, fstate,
-    wb, wof, x1, x2, nb, pj, qb, kb, vb, al, pre, run, tsum, ho, ho2s, ho2, yb, st, fs,
+    last, x_in, fresh, state_in, w_in, wo_in, gain_in, hgain_in, out, fstate,
+    wb, wof, x1, x2, nb, pj, qb, kb, vb, al, pre, run, tsum, ho, ho2s, ho2, yb, st, gain, hgain,
     ss, rs, ls,
 ):
     s = lax.axis_index("section")
@@ -96,6 +97,11 @@
         fd = 1 if e in (0, 3) else 3
         k2 = yr(4 - fd) * 4 + xr(4 - e)
         define(("F", e), wb.at[k2], wb.at[k2], dy(fd))
+        for d in SIDES:
+            v = wof.at[k, :, cols(x, 512)]
+            define(("K", e, d), v, v, dy(d))
+        v = wof.at[k2, :, cols(x, 512)]
+        define(("KF", e), v, v, dy(fd))
     for d in SIDES:
         for h in range(2):
             v = x1.at[x, pl.ds(h * 64, 64)]
@@ -107,7 +113,7 @@
         define(("CF", d), v, v, dx(d))
         v = wof.at[y * 4 + xr(4 - d), pl.ds(h * 32, 32)]
         define(("DF", d), v, v, dx(d))
-    for c in range(4):
+    for c in range(1, 4):
         for d in SIDES:
             for h in range(2):
                 v = wof.at[pl.ds(y * 4 + 2 * h, 2), :, cols(xr(c), 512)]
@@ -120,7 +126,7 @@
             define(("T", t, d), tsum.at[t, y], tsum.at[t, y], dy(d))
         define(("R", d), fresh.at[:, cols(xr(d), 512)], x2.at[xr(d), rows(x)], dx(d))
         define(("H2", d), ho2s.at[rows(xr(d))], ho2.at[x], dx(d))
-        define(("S", d), fs.at[pl.ds(2 * x, 2)], fs.at[pl.ds(2 * x, 2)], dx(d))
+        define(("S", d), fstate.at[pl.ds(2 * x, 2)], fstate.at[pl.ds(2 * x, 2)], dx(d))
     for b in range(4):
         rb = pl.ds(b * 128, 128)
         for d in SIDES:
@@ -143,9 +149,11 @@
     loads.append(pltpu.make_async_copy(x_in, x1.at[x], ls.at[3]))
     loads.append(pltpu.make_async_copy(wo_in, wof.at[r], ls.at[4]))
     loads.append(pltpu.make_async_copy(state_in.at[pl.ds(2 * x, 2)], st, ls.at[5]))
+    loads.append(pltpu.make_async_copy(gain_in, gain, ls.at[6]))
+    loads.append(pltpu.make_async_copy(hgain_in, hgain, ls.at[7]))
     for c in loads:
         c.start()
-    own_fresh = pltpu.make_async_copy(fresh.at[:, cols(x, 512)], x2.at[x, rows(x)], ls.at[6])
+    own_fresh = pltpu.make_async_copy(fresh.at[:, cols(x, 512)], x2.at[x, rows(x)], ls.at[8])
 
     barrier = pltpu.get_barrier_semaphore()
     before, after = (lax.rem(s + last, last + 1), r), (lax.rem(s + 1, last + 1), r)
@@ -163,7 +171,7 @@
             for p in range(4):
                 nb[p, to, :] = n[:, p * 512:(p + 1) * 512]
             return carry
-        lax.fori_loop(0, 8, strip, 0)
+        lax.fori_loop(0, 8, strip, 0, unroll=4)
 
     def norm_second(b):
         def strip(i, carry):
@@ -174,7 +182,7 @@
             for p in range(4):
                 nb[p, at, :] = (v[p] * scale * gain[:, p * 512:(p + 1) * 512]).astype(BF16)
             return carry
-        lax.fori_loop(0, 8, strip, 0)
+        lax.fori_loop(0, 8, strip, 0, unroll=4)
 
     def project_slice(kg, first):
         for n in range(3):
@@ -249,12 +257,6 @@
     def zero_run():
         run[...] = jnp.zeros_like(run)
 
-    def loop(f):
-        def step(b, carry):
-            f(b)
-            return carry
-        lax.fori_loop(0, 4, step, 0)
-
     for d in (1, 3, 2):
         for p in range(3):
             start("A", d, p)
@@ -263,6 +265,7 @@
     for d in SIDES:
         start("B", 0, d)
     loads[3].wait()
+    loads[6].wait()
     norm_first(x)
     for e in (1, 3):
         for p in range(3):
@@ -287,9 +290,6 @@
     start("CF", 1)
     got("C", 3, 1)
     start("CF", 3)
-    loads[4].wait()
-    for d, h in ((1, 0), (3, 1), (1, 1), (3, 0)):
-        start("D", d, h)
     forward_w(3)
     forward_w(2)
     got("C", 1, 1)
@@ -298,19 +298,13 @@
     norm_first(xr(1))
     for e in range(4):
         got("B", e, 3 if e in (0, 3) else 1)
-    got("D", 1, 0)
-    start("DF", 1)
-    got("D", 3, 1)
-    start("DF", 3)
-
-    @pl.when(s == 0)
-    def _():
-        own_fresh.start()
-        for d in (1, 3, 2):
-            start("R", d)
-
     got("CF", 1)
     got("CF", 3)
+    loads[4].wait()
+    for d, h in ((1, 0), (3, 1), (1, 1), (3, 0)):
+        start("D", d, h)
+    for d in SIDES:
+        start("K", 0, d)
     norm_first(xr(2))
     project_slice(y, True)
     project_slice(yr(3), False)
@@ -320,31 +314,51 @@
     project_slice(yr(2), False)
 
     zero_run()
-    loop(states)
+    for b in range(4):
+        states(b)
     send_totals(0)
+    got("D", 1, 0)
+    start("DF", 1)
+    got("D", 3, 1)
+    start("DF", 3)
     got("D", 1, 1)
+    for d in SIDES:
+        start("K", 1, d)
     got("D", 3, 0)
+    for d in SIDES:
+        start("K", 3, d)
+
+    def forward_k(e):
+        got("K", e, 1 if e in (0, 3) else 3)
+        start("KF", e)
+
+    forward_k(0)
+
+    @pl.when(s == 0)
+    def _():
+        own_fresh.start()
+        for d in (1, 3, 2):
+            start("R", d)
+
+    for b in range(4):
+        local(b)
+    loads[5].wait()
+    loads[7].wait()
+    base_of(0)
+
+    def put_first(rb, at, v):
+        ho[x, rb, at] = v
+
+    for b in range(4):
+        finish(b, put_first)
+        for d in SIDES:
+            start("H", b, d)
     got("DF", 1)
     got("DF", 3)
-    for d, h in ((1, 0), (3, 1), (1, 1), (3, 0)):
-        start("E", 0, d, h)
-    loop(local)
-    loads[5].wait()
-    base_of(0)
-
-    def put_first(rb, at, v):
-        ho[x, rb, at] = v
-
-    for b in range(4):
-        finish(b, put_first)
-        for d in SIDES:
-            start("H", b, d)
-    got("E", 0, 1, 0)
-    start("EF", 0, 1)
-    got("E", 0, 3, 1)
-    start("EF", 0, 3)
-    got("E", 0, 1, 1)
-    got("E", 0, 3, 0)
+    for d in SIDES:
+        start("K", 2, d)
+    for e in (1, 3, 2):
+        forward_k(e)
     for c in range(1, 4):
         for d, h in ((1, 0), (3, 1), (1, 1), (3, 0)):
             start("E", c, d, h)
@@ -396,8 +410,9 @@
 
     forward_h(0)
     forward_h(1)
-    got("EF", 0, 1)
-    got("EF", 0, 3)
+    for e in range(4):
+        got("K", e, 3 if e in (0, 3) else 1)
+        got("KF", e)
     out_first(0)
     forward_h(2)
     out_first(1)
@@ -424,9 +439,10 @@
     second(3)
 
     send_totals(1)
-    loop(local)
+    for b in range(4):
+        local(b)
     base_of(1)
-    fs[pl.ds(2 * x, 2)] = st[...].astype(BF16)
+    fstate[pl.ds(2 * x, 2)] = st[...].astype(BF16)
 
     def put_second(rb, at, v):
         ho2s[rb, at] = v
@@ -457,7 +473,6 @@
         out[:, at] = v.astype(BF16)
     for d in (1, 3, 2):
         got("S", d)
-    fstate[...] = fs[...].astype(F32)
 
     for key in IDS:
         if key[0] == "Z":
@@ -481,9 +496,9 @@
         name="two_ticks",
         out_shape=(
             jax.ShapeDtypeStruct((128, 2048), BF16),
-            jax.ShapeDtypeStruct((8, 128, 128), F32),
+            jax.ShapeDtypeStruct((8, 128, 128), BF16),
         ),
-        in_specs=[anywhere] * 5 + [vmem] * 2,
+        in_specs=[anywhere] * 7,
         out_specs=(vmem, vmem),
         scratch_shapes=[
             pltpu.VMEM((16, 128, 768), BF16),
@@ -504,19 +519,20 @@
             pltpu.VMEM((4, 128, 256), BF16),
             pltpu.VMEM((512, 512), BF16),
             pltpu.VMEM((2, 128, 128), F32),
-            pltpu.VMEM((8, 128, 128), BF16),
+            pltpu.VMEM((1, 2048), F32),
+            pltpu.VMEM((1, 1024), F32),
             pltpu.SemaphoreType.DMA((n,)),
             pltpu.SemaphoreType.DMA((n,)),
-            pltpu.SemaphoreType.DMA((7,)),
+            pltpu.SemaphoreType.DMA((9,)),
         ],
         compiler_params=pltpu.CompilerParams(
-            collective_id=0, has_side_effects=True, vmem_limit_bytes=48 * 2**20
+            collective_id=0, has_side_effects=True, vmem_limit_bytes=61 * 2**20
         ),
         cost_estimate=pl.CostEstimate(flops=4_600_000_000, bytes_accessed=4_000_000, transcendentals=0),
     )(
         section_inputs[0], fresh_group, resident_state[0], qkv_weight[0], out_weight[0], input_gain, head_gain
     )
-    return (out[None], state[None])
+    return (out[None], state.astype(F32)[None])
 
 
 def solution(mesh):

time: 109 us -> 102 us (0.936)
  local copies, waits for them, and re-layouts: 8.17 us -> 0.8 us
  other arithmetic: 0 us -> 1.84 us
  Pallas kernels: 99.9 us -> 98.5 us
    unnamed x16 -> x3, local copies, waits for them, and re-layouts: 8.17 us -> 0.8 us
    broadcast_in_dim x0 -> x1, other arithmetic: none -> 1.84 us  [body(): return (out[None], state.astype(F32)[None])]
    pallas_call x1, Pallas kernels: 99.9 us -> 98.5 us  [body(): pl.pallas_call(functools.partial(kernel, lax.axis_size('section') - 1), n...]
where the time goes in v3:
time: 102 us
  Pallas kernels  98.5 us (97%)
  other arithmetic  1.84 us (2%)
    pallas_call x1, Pallas kernels, body(): pl.pallas_call(functools.partial(kernel, lax.axis_size('section') - 1), n...  98.5 us

profile of v3, /device:TPU:1, one launch (start us, length us, event | category | flops | bytes accessed | tf_op | source)
XLA Modules:
  0.0 101.8 jit_solution(486965809524211560)
XLA Ops:
  0.6 98.5 %two_ticks.1 = (bf16[128,2048]{1,0:T(8,128)(2,1)}, bf16[8,128,128]{2,1,0:T(8,128)(2,1)}) custom-call(bf16[128,2048]{1,0:T(8,128)(2,1)} %bitcast.10, bf16[128,2048]{1,0:T(8,128)(2,1)} %fresh.1, f32[8,128,128]{2,1,0:T(8,128)} %bitcast.11, bf16[128,3072]{1,0:T(8,128)(2,1)} %bitcast.9, bf16[64,2048]{1,0:T(8,128)(2,1)} %bitcast.12, f32[1,2048]{1,0:T(1,128)} %gain_in.1, ...), custom_call_target="tpu_custom_call" | custom-call | flops 4600000000 | bytes 4000000 | tf_op jit(solution)/shard_map/two_ticks/pallas_call | solution.py:494
  99.1 0.0 copy-start
  99.1 1.8 %bitcast_convert_fusion = f32[1,8,128,128]{3,2,1,0:T(8,128)} fusion(bf16[8,128,128]{2,1,0:T(8,128)(2,1)} %get-tuple-element.5), kind=kLoop, calls=%fused_computation | loop fusion | flops 131072 | bytes 786432 | tf_op jit(solution)/shard_map/broadcast_in_dim | solution.py:535
  101.0 0.0 copy-done
  101.0 0.8 copy.10
Async XLA Ops:
  99.1 1.8 %copy-start = (bf16[128,2048]{1,0:T(8,128)(2,1)S(1)}, bf16[128,2048]{1,0:T(8,128)(2,1)}, u32[]{:S(2)}) copy-start(bf16[128,2048]{1,0:T(8,128)(2,1)} %get-tuple-element.4) | copy-start | bytes 1572868

commit v4 on v3

--- a/solution.py
+++ b/solution.py
@@ -37,7 +37,7 @@
         slot("H", _b, _d), slot("G", _b, _d)
     slot("HF", _b), slot("GF", _b), slot("Z", _b)
 for _d in (1, 2, 3):
-    slot("T", 0, _d), slot("T", 1, _d), slot("R", _d), slot("H2", _d), slot("S", _d)
+    slot("T", 0, _d), slot("T", 1, _d), slot("R", _d), slot("H2", _d), slot("S", _d), slot("U", _d)
 
 
 def kernel(
@@ -68,6 +68,7 @@
     def cols(j, n):
         return pl.ds(pl.multiple_of(j * n, n), n)
 
+    quarter = pl.ds(pl.multiple_of(32 * y, 32), 32)
     makers = {}
 
     def define(key, src, dst, dev):
@@ -126,7 +127,10 @@
             define(("T", t, d), tsum.at[t, y], tsum.at[t, y], dy(d))
         define(("R", d), fresh.at[:, cols(xr(d), 512)], x2.at[xr(d), rows(x)], dx(d))
         define(("H2", d), ho2s.at[rows(xr(d))], ho2.at[x], dx(d))
-        define(("S", d), fstate.at[pl.ds(2 * x, 2)], fstate.at[pl.ds(2 * x, 2)], dx(d))
+        v = fstate.at[pl.ds(2 * x, 2), quarter]
+        define(("S", d), v, v, dx(d))
+        v = fstate.at[:, quarter]
+        define(("U", d), v, v, dy(d))
     for b in range(4):
         rb = pl.ds(b * 128, 128)
         for d in SIDES:
@@ -442,7 +446,9 @@
     for b in range(4):
         local(b)
     base_of(1)
-    fstate[pl.ds(2 * x, 2)] = st[...].astype(BF16)
+    fstate[pl.ds(2 * x, 2), quarter] = st[:, quarter].astype(BF16)
+    for d in (2, 1, 3):
+        start("S", d)
 
     def put_second(rb, at, v):
         ho2s[rb, at] = v
@@ -450,12 +456,14 @@
     for d in (2, 1, 3):
         finish(xr(d), put_second)
         start("H2", d)
-    for d in (2, 1, 3):
-        start("S", d)
 
     def put_own(rb, at, v):
         ho2[x, :, at] = v
 
+    for d in (2, 1, 3):
+        got("S", d)
+    for d in (2, 1, 3):
+        start("U", d)
     finish(x, put_own)
     for c in range(1, 4):
         got("E", c, 1, 1)
@@ -472,7 +480,7 @@
             v += jnp.dot(ho2[j], w, preferred_element_type=F32)
         out[:, at] = v.astype(BF16)
     for d in (1, 3, 2):
-        got("S", d)
+        got("U", d)
 
     for key in IDS:
         if key[0] == "Z":

time: 102 us -> 102 us (level)
  no operation moved by 1% of the time
where the time goes in v4:
time: 102 us; the launch traced here: 101 us
  Pallas kernels  98.2 us (96%)
  other arithmetic  1.84 us (2%)
    pallas_call x1, Pallas kernels, body(): pl.pallas_call(functools.partial(kernel, lax.axis_size('section') - 1), n...  98.2 us

profile of v4, /device:TPU:1, one launch (start us, length us, event | category | flops | bytes accessed | tf_op | source)
XLA Modules:
  0.0 101.5 jit_solution(6405485392276830216)
XLA Ops:
  0.6 98.2 %two_ticks.1 = (bf16[128,2048]{1,0:T(8,128)(2,1)}, bf16[8,128,128]{2,1,0:T(8,128)(2,1)}) custom-call(bf16[128,2048]{1,0:T(8,128)(2,1)} %bitcast.10, bf16[128,2048]{1,0:T(8,128)(2,1)} %fresh.1, f32[8,128,128]{2,1,0:T(8,128)} %bitcast.11, bf16[128,3072]{1,0:T(8,128)(2,1)} %bitcast.9, bf16[64,2048]{1,0:T(8,128)(2,1)} %bitcast.12, f32[1,2048]{1,0:T(1,128)} %gain_in.1, ...), custom_call_target="tpu_custom_call" | custom-call | flops 4600000000 | bytes 4000000 | tf_op jit(solution)/shard_map/two_ticks/pallas_call | solution.py:502
  98.8 0.0 copy-start
  98.8 1.8 %bitcast_convert_fusion = f32[1,8,128,128]{3,2,1,0:T(8,128)} fusion(bf16[8,128,128]{2,1,0:T(8,128)(2,1)} %get-tuple-element.5), kind=kLoop, calls=%fused_computation | loop fusion | flops 131072 | bytes 786432 | tf_op jit(solution)/shard_map/broadcast_in_dim | solution.py:543
  100.7 0.0 copy-done
  100.7 0.8 copy.10
Async XLA Ops:
  98.8 1.8 %copy-start = (bf16[128,2048]{1,0:T(8,128)(2,1)S(1)}, bf16[128,2048]{1,0:T(8,128)(2,1)}, u32[]{:S(2)}) copy-start(bf16[128,2048]{1,0:T(8,128)(2,1)} %get-tuple-element.4) | copy-start | bytes 1572868

commit v5 on v3

--- a/solution.py
+++ b/solution.py
@@ -295,16 +295,16 @@
     got("C", 1, 1)
     norm_first(xr(3))
     got("C", 3, 0)
+    loads[4].wait()
+    for d, h in ((1, 0), (3, 1), (1, 1), (3, 0)):
+        start("D", d, h)
+    for d in SIDES:
+        start("K", 0, d)
     norm_first(xr(1))
     for e in range(4):
         got("B", e, 3 if e in (0, 3) else 1)
     got("CF", 1)
     got("CF", 3)
-    loads[4].wait()
-    for d, h in ((1, 0), (3, 1), (1, 1), (3, 0)):
-        start("D", d, h)
-    for d in SIDES:
-        start("K", 0, d)
     norm_first(xr(2))
     project_slice(y, True)
     project_slice(yr(3), False)

time: 102 us -> 102 us (level)
  no operation moved by 1% of the time
where the time goes in v5:
time: 102 us; the launch traced here: 101 us
  Pallas kernels  98.1 us (96%)
  other arithmetic  1.84 us (2%)
    pallas_call x1, Pallas kernels, body(): pl.pallas_call(functools.partial(kernel, lax.axis_size('section') - 1), n...  98.1 us

profile of v5, /device:TPU:1, one launch (start us, length us, event | category | flops | bytes accessed | tf_op | source)
XLA Modules:
  0.0 101.4 jit_solution(788758804675375498)
XLA Ops:
  0.6 98.1 %two_ticks.1 = (bf16[128,2048]{1,0:T(8,128)(2,1)}, bf16[8,128,128]{2,1,0:T(8,128)(2,1)}) custom-call(bf16[128,2048]{1,0:T(8,128)(2,1)} %bitcast.10, bf16[128,2048]{1,0:T(8,128)(2,1)} %fresh.1, f32[8,128,128]{2,1,0:T(8,128)} %bitcast.11, bf16[128,3072]{1,0:T(8,128)(2,1)} %bitcast.9, bf16[64,2048]{1,0:T(8,128)(2,1)} %bitcast.12, f32[1,2048]{1,0:T(1,128)} %gain_in.1, ...), custom_call_target="tpu_custom_call" | custom-call | flops 4600000000 | bytes 4000000 | tf_op jit(solution)/shard_map/two_ticks/pallas_call | solution.py:494
  98.7 0.0 copy-start
  98.7 1.8 %bitcast_convert_fusion = f32[1,8,128,128]{3,2,1,0:T(8,128)} fusion(bf16[8,128,128]{2,1,0:T(8,128)(2,1)} %get-tuple-element.5), kind=kLoop, calls=%fused_computation | loop fusion | flops 131072 | bytes 786432 | tf_op jit(solution)/shard_map/broadcast_in_dim | solution.py:535
  100.6 0.0 copy-done
  100.6 0.8 copy.10
Async XLA Ops:
  98.7 1.8 %copy-start = (bf16[128,2048]{1,0:T(8,128)(2,1)S(1)}, bf16[128,2048]{1,0:T(8,128)(2,1)}, u32[]{:S(2)}) copy-start(bf16[128,2048]{1,0:T(8,128)(2,1)} %get-tuple-element.4) | copy-start | bytes 1572868
